TPU v7x, 32 devices: a whole 2x2x4 slice. The times are simulated.
32 devices in a mesh: leaf: 8 (over z, y), panel: 4 (over x, core).
Axes of the slice: x: 2, y: 2, z: 4, core: 2. Of those that a mesh axis runs over, the one named last changes fastest.
Arguments:
- right_sides: float32 [7, 4096, 512], P(None, 'leaf', 'panel'), may hold values from -11 to 11
- inverse_diagonal: bfloat16 [7, 4096, 4096], P(None, 'leaf'), may hold values from -1 to 2, as said below
- off_diagonal: bfloat16 [6, 4096, 4096], P(None, 'leaf'), may hold values from -0.0625 to 0.0625
- structure: int32 [6, 32], replicated, may hold values from 0 to 95, as said below
- pivot_counts: int32 [7], replicated, may hold values from 2048 to 4096, as said below
Outputs:
- samples: float32 [7, 4096, 512], P(None, 'leaf', 'panel')
- sample_power: float32 [7, 4096], P(None, 'leaf')
Inputs may be any that keep to these rules, and one draw needn't show every extreme that they name: `inverse_diagonal`: zero below the diagonal; diagonal entries positive. `structure`: a front of the middle level lists 4096 // 128 distinct blocks of the root (numbers below 32); a bottom front lists distinct blocks of the root and of its parent (parent p = 1 + (f - 3) // 2 holds block numbers p * 32 to (p + 1) * 32 - 1). `pivot_counts`: rows from the count on are padding; some front has exactly 4096 live rows and some exactly 2048.
All inputs are finite; a program needn't handle non-finite values.
Results may differ from a plain program's by a relative error of at most 0.0038.
Values may be sent and summed in bfloat16 or wider, within the bound.
A program may use at most 128 MiB of HBM per device.

v0:
```python
import jax
import jax.numpy as jnp
from jax import lax
from jax.sharding import PartitionSpec as P


def share_rows(stored_rows):
    return lax.all_gather(stored_rows, "leaf", axis=1, tiled=True)


def solve_fronts(rhs_block, update, inverse, live_mask):
    reduced = (live_mask * (rhs_block - update)).astype(jnp.bfloat16)
    running = jnp.einsum(
        "fij,fjr->fir",
        inverse,
        lax.all_gather(reduced, "leaf", axis=1, tiled=True),
        preferred_element_type=jnp.float32,
    )
    return live_mask * running


def couple(blocks, picked):
    return jnp.einsum("fik,fkr->fir", blocks, picked, preferred_element_type=jnp.float32)


def local(right_sides, inverse_diagonal, off_diagonal, structure, pivot_counts):
    rows_local = right_sides.shape[1]
    columns_dev = right_sides.shape[2]
    pivot_rows = inverse_diagonal.shape[2]
    coupled = off_diagonal.shape[2]
    block_size = coupled // structure.shape[1]
    first_row = lax.axis_index("leaf") * rows_local
    position = first_row + jnp.arange(rows_local, dtype=jnp.int32)
    live_rows = (position[None, :] < pivot_counts[:, None]).astype(jnp.float32)[:, :, None]
    wanted = (
        structure[:, :, None] * block_size + jnp.arange(block_size, dtype=jnp.int32)[None, None, :]
    ).reshape(6, coupled)
    pieces = 1
    block_width = columns_dev // pieces
    root_solved = solve_fronts(
        right_sides[0:1], jnp.zeros_like(right_sides[0:1]), inverse_diagonal[0:1], live_rows[0:1]
    )
    root_all = share_rows(root_solved.astype(jnp.bfloat16))[0]
    middle_update = couple(off_diagonal[0:2], jnp.take(root_all, wanted[0:2], axis=0))
    middle = solve_fronts(right_sides[1:3], middle_update, inverse_diagonal[1:3], live_rows[1:3])
    middle_all = share_rows(middle.astype(jnp.bfloat16)).reshape(2 * pivot_rows, block_width)
    ancestors = jnp.concatenate([root_all, middle_all], axis=0)
    bottom_update = couple(off_diagonal[2:6], jnp.take(ancestors, wanted[2:6], axis=0))
    bottom = solve_fronts(right_sides[3:7], bottom_update, inverse_diagonal[3:7], live_rows[3:7])
    results = jnp.concatenate([root_solved, middle, bottom], axis=0)
    squares = lax.psum(jnp.sum(results * results, axis=2), "panel")
    sample_power = squares / jnp.float32(columns_dev * lax.axis_size("panel"))
    return (results, sample_power)


def solution(mesh):
    placed = (P(None, "leaf", "panel"), P(None, "leaf", None), P(None, "leaf", None), P(), P())
    return jax.shard_map(
        local,
        mesh=mesh,
        in_specs=placed,
        out_specs=(P(None, "leaf", "panel"), P(None, "leaf")),
        check_vma=False,
    )
```

profile of v0, /device:TPU:0, one launch (start us, length us, event | category | flops | bytes accessed | tf_op | source)
XLA Modules:
  0.0 417.3 jit_solution(8191169920169745915)
XLA Ops:
  7.2 0.0 copy-start.2
  7.2 0.0 all-gather.7.cloned.1.call-start
  7.2 0.7 compare_convert_fusion
  8.0 1.7 multiply_convert_fusion
  9.7 0.0 all-gather.7.cloned.1.call-update
  9.7 0.0 slice-start
  9.7 0.0 all-gather.15.cloned.1.call-start
  9.8 43.8 %all-gather.7.cloned.1.call-done = bf16[1,4096,128]{2,1,0:T(8,128)(2,1)} async-done(((bf16[1,512,128]{2,1,0:T(8,128)(2,1)}), bf16[1,4096,128]{2,1,0:T(8,128)(2,1)}) %all-gather.7.cloned.1.call-update) | async-done | bytes 1048592 | tf_op jit(solution)/shard_map/all_gather | solution.py:16
  53.6 4.8 %bitcast_convert_fusion = (bf16[512,128]{0,1:T(8,128)(2,1)}, f32[128,512]{1,0:T(8,128)}) fusion(bf16[7,512,4096]{2,1,0:T(8,128)(2,1)} %param.6, bf16[1,4096,128]{2,1,0:T(8,128)(2,1)} %all-gather.7.cloned.1.call-done, f32[512]{0:T(512)S(1)} %bitcast.67), kind=kOutput, calls=%fused_computation.36 | convolution fusion | flops 537001984 | bytes 5638144 | tf_op jit(solution)/shard_map/fij,fjr->fir/dot_general | solution.py:13
  58.4 0.0 all-gather.15.cloned.1.call-update
  58.4 0.0 all-gather.9.cloned.1.call-start
  58.5 0.0 copy-done.2
  58.5 0.1 iota_add_fusion
  58.7 0.0 slice-done
  58.7 1.0 copy.18
  59.7 37.1 %all-gather.15.cloned.1.call-done = bf16[4096,128]{0,1:T(8,128)(2,1)} async-done(((bf16[512,128]{0,1:T(8,128)(2,1)}), bf16[4096,128]{0,1:T(8,128)(2,1)}) %all-gather.15.cloned.1.call-update) | async-done | bytes 1048592 | tf_op jit(solution)/shard_map/all_gather | solution.py:8
  96.9 1.6 copy.13
  98.5 0.0 copy-start
  98.5 24.0 %gather_fusion = bf16[8192,128]{1,0:T(8,128)(2,1)S(1)} fusion(bf16[4096,128]{1,0:T(8,128)(2,1)S(1)} %copy.13, s32[8192]{0:T(1024)S(1)} %broadcast_clamp_fusion.1), kind=kCustom, calls=%fused_computation | custom fusion | bytes 4227072 | tf_op jit(solution)/shard_map/jit(_take)/gather | solution.py:44
  122.5 0.0 copy-done
  122.5 6.8 %fusion.63 = bf16[2,512,128]{1,2,0:T(8,128)(2,1)} fusion(f32[2,512,128]{1,2,0:T(8,128)} %copy.18, bf16[6,512,4096]{2,1,0:T(8,128)(2,1)} %param.7, bf16[2,4096,128]{2,1,0:T(8,128)(2,1)S(1)} %bitcast.62, pred[2,4096]{1,0:T(4,128)(4,1)S(1)} %compare_and_fusion.1, f32[2,512]{1,0:T(2,128)S(1)} %slice.74), kind=kOutput, calls=%fused_computation.32 | convolution fusion | flops 1075183616 | bytes 11284480 | tf_op jit(solution)/shard_map/fik,fkr->fir/dot_general | solution.py:23
  129.3 0.0 all-gather.9.cloned.1.call-update
  129.4 0.0 slice-start.1
  129.4 0.0 all-gather.11.cloned.1.call-start
  129.4 50.0 %all-gather.9.cloned.1.call-done = bf16[2,4096,128]{1,2,0:T(8,128)(2,1)} async-done(((bf16[2,512,128]{1,2,0:T(8,128)(2,1)}), bf16[2,4096,128]{1,2,0:T(8,128)(2,1)}) %all-gather.9.cloned.1.call-update) | async-done | bytes 2097168 | tf_op jit(solution)/shard_map/all_gather | solution.py:16
  179.5 7.8 %fusion.77 = (bf16[2,512,128]{1,2,0:T(8,128)(2,1)}, f32[2,512,128]{1,2,0:T(8,128)}) fusion(bf16[2,4096,128]{1,2,0:T(8,128)(2,1)} %all-gather.9.cloned.1.call-done, bf16[7,512,4096]{2,1,0:T(8,128)(2,1)} %param.6, f32[2,512]{1,0:T(2,128)S(1)} %slice.74), kind=kOutput, calls=%fused_computation.57 | convolution fusion | flops 1074003968 | bytes 11276288 | tf_op jit(solution)/shard_map/fij,fjr->fir/dot_general | solution.py:13
  187.3 0.0 all-gather.11.cloned.1.call-update
  187.3 0.0 all-gather.13.cloned.1.call-start
  187.5 0.0 slice-done.1
  187.5 1.3 copy.19
  188.8 0.1 compare_and_fusion
  188.9 47.8 %all-gather.11.cloned.1.call-done = bf16[2,4096,128]{1,2,0:T(8,128)(2,1)} async-done(((bf16[2,512,128]{1,2,0:T(8,128)(2,1)}), bf16[2,4096,128]{1,2,0:T(8,128)(2,1)}) %all-gather.11.cloned.1.call-update) | async-done | bytes 2097168 | tf_op jit(solution)/shard_map/all_gather | solution.py:8
  236.7 4.1 copy.15
  240.8 2.8 pad_maximum_fusion
  243.6 57.4 %gather_fusion.1 = bf16[16384,128]{1,0:T(8,128)(2,1)} fusion(bf16[12288,128]{1,0:T(8,128)(2,1)S(1)} %pad_maximum_fusion, s32[16384]{0:T(1024)S(1)} %broadcast_clamp_fusion), kind=kCustom, calls=%fused_computation.1 | custom fusion | bytes 8454144 | tf_op jit(solution)/shard_map/jit(_take)/gather | solution.py:48
  301.0 11.7 %fusion.37 = bf16[4,512,128]{1,2,0:T(8,128)(2,1)} fusion(f32[4,512,128]{1,2,0:T(8,128)} %copy.19, bf16[6,512,4096]{2,1,0:T(8,128)(2,1)} %param.7, bf16[4,4096,128]{2,1,0:T(8,128)(2,1)} %bitcast.61, pred[4,4096]{1,0:T(4,128)(4,1)S(1)} %compare_and_fusion, f32[4,512]{1,0:T(4,128)S(1)} %slice.76), kind=kOutput, calls=%fused_computation.26 | convolution fusion | flops 2150367232 | bytes 22568960 | tf_op jit(solution)/shard_map/fik,fkr->fir/dot_general | solution.py:23
  312.8 0.0 all-gather.13.cloned.1.call-update
  312.8 0.0 copy-start.1
  312.8 73.3 %all-gather.13.cloned.1.call-done = bf16[4,4096,128]{1,2,0:T(8,128)(2,1)} async-done(((bf16[4,512,128]{1,2,0:T(8,128)(2,1)}), bf16[4,4096,128]{1,2,0:T(8,128)(2,1)}) %all-gather.13.cloned.1.call-update) | async-done | bytes 4194320 | tf_op jit(solution)/shard_map/all_gather | solution.py:16
  386.1 10.6 %fusion.34 = f32[4,512,128]{1,2,0:T(8,128)S(1)} fusion(bf16[4,4096,128]{1,2,0:T(8,128)(2,1)} %all-gather.13.cloned.1.call-done, bf16[7,512,4096]{2,1,0:T(8,128)(2,1)} %param.6, f32[4,512]{1,0:T(4,128)S(1)} %slice.76), kind=kOutput, calls=%fused_computation.25 | convolution fusion | flops 2147745792 | bytes 22028288 | tf_op jit(solution)/shard_map/fij,fjr->fir/dot_general | solution.py:13
  396.7 0.0 copy-done.1
  396.7 1.3 multiply_reduce_fusion
  398.0 1.7 copy.17
  399.7 10.5 %psum.7 = f32[7,512]{1,0:T(8,128)S(1)} all-reduce(f32[7,512]{1,0:T(8,128)S(1)} %get-tuple-element.6), channel_id=1, replica_groups=mesh['leaf'=8,'panel'=4] {'panel'}, use_global_device_ids=true, to_apply=%region_1.2 | all-reduce | flops 3584 | bytes 28672 | tf_op jit(solution)/shard_map/psum | solution.py:51
  410.2 0.6 broadcast_multiply_fusion
  (16 shorter events, 0.2 us)
Async XLA Ops:
  7.2 51.3 %copy-start.2 = (s32[6,32]{1,0:T(8,128)S(1)}, s32[6,32]{1,0:T(8,128)}, u32[]{:S(2)}) copy-start(s32[6,32]{1,0:T(8,128)} %param.8) | copy-start | bytes 2308
  7.2 46.4 %all-gather.7.cloned.1.call-start = ((), (), s32[]{:S(2)}) async-start(), calls=%async_computation | async-start | bytes 1179648 | tf_op jit(solution)/shard_map/all_gather | solution.py:16
  9.7 48.9 %slice-start = ((f32[7,512,128]{2,1,0:T(8,128)}), f32[2,512,128]{2,1,0:T(8,128)S(1)}, s32[]{:S(2)}) async-start(f32[7,512,128]{2,1,0:T(8,128)} %param.5), calls=%async_computation.5 | async-start | bytes 1048576 | tf_op jit(solution)/shard_map/slice | solution.py:45
  9.7 87.1 %all-gather.15.cloned.1.call-start = ((), (), s32[]{:S(2)}) async-start(), calls=%async_computation.4 | async-start | bytes 1179648 | tf_op jit(solution)/shard_map/all_gather | solution.py:8
  58.4 121.1 %all-gather.9.cloned.1.call-start = ((), (), s32[]{:S(2)}) async-start(), calls=%async_computation.1 | async-start | bytes 2359296 | tf_op jit(solution)/shard_map/all_gather | solution.py:16
  98.5 24.1 %copy-start = (bf16[4096,128]{1,0:T(8,128)(2,1)}, bf16[4096,128]{1,0:T(8,128)(2,1)S(1)}, u32[]{:S(2)}) copy-start(bf16[4096,128]{1,0:T(8,128)(2,1)S(1)} %copy.13) | copy-start | bytes 3145732
  129.4 58.1 %slice-start.1 = ((f32[7,512,128]{2,1,0:T(8,128)}), f32[4,512,128]{2,1,0:T(8,128)S(1)}, s32[]{:S(2)}) async-start(f32[7,512,128]{2,1,0:T(8,128)} %param.5), calls=%async_computation.6 | async-start | bytes 2097152 | tf_op jit(solution)/shard_map/slice | solution.py:49
  129.4 107.4 %all-gather.11.cloned.1.call-start = ((), (), s32[]{:S(2)}) async-start(), calls=%async_computation.2 | async-start | bytes 2359296 | tf_op jit(solution)/shard_map/all_gather | solution.py:8
  187.3 198.8 %all-gather.13.cloned.1.call-start = ((), (), s32[]{:S(2)}) async-start(), calls=%async_computation.3 | async-start | bytes 4718592 | tf_op jit(solution)/shard_map/all_gather | solution.py:16
  312.8 83.9 %copy-start.1 = (f32[2,512,128]{1,2,0:T(8,128)S(1)}, f32[2,512,128]{1,2,0:T(8,128)}, u32[]{:S(2)}) copy-start(f32[2,512,128]{1,2,0:T(8,128)} %get-tuple-element.15) | copy-start | bytes 1572868
Sparse Core Ops, SparseCore 0:
  10.7 42.8 all-gather.6
  58.5 38.2 all-gather.14
  129.5 49.9 all-gather.8
  187.5 49.2 all-gather.10
  312.9 73.1 all-gather.12
where the time goes:
time: 418 us; the launch traced here: 417 us
  waiting for transfers between devices  252 us (60%)
  local copies, waits for them, and re-layouts  91.2 us (22%)
  matrix products  41.7 us (10%)
  between operations  14 us (3%)
  blocking collectives  10.5 us (3%)
  other arithmetic  7.43 us (2%)
    all_gather x3, waiting for transfers between devices, solve_fronts(): lax.all_gather(reduced, 'leaf', axis=1, tiled=True)  167 us
    all_gather x2, waiting for transfers between devices, share_rows(): return lax.all_gather(stored_rows, 'leaf', axis=1, tiled=True)  85 us
    gather x1, local copies, waits for them, and re-layouts, local(): jnp.take(ancestors, wanted[2:6], axis=0)  57.4 us
    gather x1, local copies, waits for them, and re-layouts, local(): jnp.take(root_all, wanted[0:2], axis=0)  24 us
    dot_general x3, matrix products, solve_fronts(): jnp.einsum('fij,fjr->fir', inverse, lax.all_gather(reduced, 'leaf', axis=...  23.2 us
    dot_general x2, matrix products, couple(): jnp.einsum('fik,fkr->fir', blocks, picked, preferred_element_type=jnp.flo...  18.5 us
    psum x1, blocking collectives, local(): squares = lax.psum(jnp.sum(results * results, axis=2), 'panel')  10.5 us
  transfers between devices with their start and end apart: 5, of which 5 were waited for; matrix products, arithmetic and copies ran while one was open for 1% of the time, Pallas kernels for 0%

commit v1 on v0

v1 whole, which is shorter than its diff:
```python
import functools
import math

import jax
import jax.numpy as jnp
from jax import lax
from jax.experimental import pallas as pl
from jax.experimental.pallas import tpu as pltpu
from jax.sharding import PartitionSpec as P

SLOTS = 8
DOWN, UP, SIDE = 0, 1, 2
MESH = pl.DeviceIdType.MESH


def kernel(
    leaves, panels, total_columns,
    rhs, inv, off, structure, counts,
    out, power,
    red, root, anc0, anc1, mats, picked, acc, sums,
    mat_sem, send_sem, recv_sem, sums_send, sums_recv,
):
    leaf = lax.axis_index("leaf")
    panel = lax.axis_index("panel")
    depth = leaves // 2
    z, y = leaf // 2, leaf % 2
    rows, columns = rhs.shape[1], rhs.shape[2]
    pivots = red.shape[1]
    coupled = off.shape[2]
    listed = structure.shape[1]
    block = coupled // listed
    pair = 2 * rows
    wide = min(coupled, 1024)
    unit = root.shape[1]
    units, piece_units = pivots // unit, rows // unit

    sequence = [(inv, 0), (off, 0), (off, 1), (inv, 1), (inv, 2)]
    sequence += [(off, 2 + i) for i in range(4)] + [(inv, 3 + i) for i in range(4)]

    def load(i):
        source, which = sequence[i]
        slot = i % SLOTS
        return pltpu.make_async_copy(source.at[which], mats.at[slot], mat_sem.at[slot])

    def release(i):
        if i + SLOTS < len(sequence):
            load(i + SLOTS).start()

    for i in range(min(SLOTS, len(sequence))):
        load(i).start()

    has_down, has_up = z > 0, z < depth - 1

    barrier = pltpu.get_barrier_semaphore()

    def greet(target):
        pl.semaphore_signal(barrier, inc=1, device_id=target, device_id_type=MESH)

    below, above, beside = leaf - 2, leaf + 2, leaf + 1 - 2 * y
    pl.when(has_down)(lambda: greet({"leaf": below}))
    pl.when(has_up)(lambda: greet({"leaf": above}))
    greet({"leaf": beside})
    for hop in range(1, panels):
        greet({"panel": lax.rem(panel + hop, panels)})
    pl.semaphore_wait(barrier, panels + has_down.astype(jnp.int32) + has_up.astype(jnp.int32))

    def rows_of(gather, piece):
        if gather < 7:
            return red.at[gather, pl.ds(pl.multiple_of(piece * rows, rows), rows)]
        if gather == 7:
            return root.at[pl.ds(piece * piece_units, piece_units)]
        return (anc0, anc1)[gather - 8].at[pl.ds(units + piece * piece_units, piece_units)]

    def transfer(gather, layer, side, way):
        piece = 2 * layer + side
        held = rows_of(gather, piece)
        return pltpu.make_async_remote_copy(
            src_ref=held,
            dst_ref=held,
            send_sem=send_sem.at[gather, way, layer],
            recv_sem=recv_sem.at[gather, piece],
            device_id={"leaf": (below, above, beside)[way]},
            device_id_type=MESH,
        )

    def send(gather, layer, way, allowed=None):
        if allowed is None:
            transfer(gather, layer, y, way).start()
        else:
            pl.when(allowed)(lambda: transfer(gather, layer, y, way).start())

    def arrived(gather, layer, side):
        transfer(gather, layer, side, SIDE).wait_recv()

    position = leaf * rows + lax.broadcasted_iota(jnp.int32, (rows, columns), 0)

    def live(front):
        return jnp.clip(counts[front] - position, 0, 1).astype(jnp.float32)

    def publish_reduced(front, update):
        value = rhs[front] if update is None else rhs[front] - update
        rows_of(front, leaf)[...] = (live(front) * value).astype(jnp.bfloat16)
        send(front, z, DOWN, has_down)
        send(front, z, SIDE)

    def couple(front, order, ancestors):
        parts = block // unit
        for i in range(listed):
            number = structure[front - 1, i]
            if ancestors is anc1:
                per_front = pivots // block
                number = jnp.minimum(number, jnp.maximum(number - per_front, per_front - 1))
            for j in range(parts):
                picked[pl.ds(i * block + j * unit, unit), :] = ancestors[number * parts + j]
        load(order).wait()
        acc[0] = jnp.zeros((rows, columns), jnp.float32)

        @pl.loop(0, coupled // wide)
        def _(i):
            start = pl.multiple_of(i * wide, wide)
            acc[0] += jnp.dot(
                mats[order % SLOTS, :, pl.ds(start, wide)],
                picked[pl.ds(start, wide), :],
                preferred_element_type=jnp.float32,
            )

        release(order)
        publish_reduced(front, acc[0])

    def finish(front):
        solved = live(front) * acc[front % 4]
        out[front] = solved
        if front < 3:
            gather = 7 + front
            rows_of(gather, leaf)[...] = solved.astype(jnp.bfloat16).reshape(piece_units, unit, columns)
            send(gather, z, DOWN, has_down)
            send(gather, z, UP, has_up)
            send(gather, z, SIDE)
        tall = min(rows, 128)
        for i in range(rows // tall):
            part = solved[i * tall:(i + 1) * tall]
            sums[panel, pl.ds(front, 1), i * tall:(i + 1) * tall] = jnp.sum(
                (part * part).T, axis=0, keepdims=True
            )

    def solve(fronts, orders):
        for front in fronts:
            acc[front % 4] = jnp.zeros((rows, columns), jnp.float32)

        @pl.loop(1, depth - z + 1)
        def _(step):
            layer = z + step

            @pl.when(layer < depth)
            def _():
                for front in fronts:
                    arrived(front, layer, y)
                    send(front, layer, DOWN, has_down)
                    send(front, layer, SIDE)

            done = layer - 1
            start = pl.multiple_of(done * pair, pair)
            for front, order in zip(fronts, orders):
                arrived(front, done, 1 - y)
                pl.when(step == 1)(lambda: load(order).wait())
                acc[front % 4] += jnp.dot(
                    mats[order % SLOTS, :, pl.ds(start, pair)],
                    red[front, pl.ds(start, pair), :],
                    preferred_element_type=jnp.float32,
                )
                pl.when(layer == depth)(lambda: finish(front))

        for order in orders:
            release(order)

    def share(fronts):
        @pl.loop(1, depth)
        def _(step):
            for front in fronts:
                gather = 7 + front

                @pl.when(z + step < depth)
                def _():
                    arrived(gather, z + step, y)
                    send(gather, z + step, DOWN, has_down)
                    send(gather, z + step, SIDE)

                @pl.when(z - step >= 0)
                def _():
                    arrived(gather, z - step, y)
                    send(gather, z - step, UP, has_up)
                    send(gather, z - step, SIDE)

    def share_end(front):
        @pl.loop(0, depth)
        def _(layer):
            arrived(7 + front, layer, 1 - y)

    publish_reduced(0, None)
    solve([0], [0])
    share([0])
    share_end(0)
    couple(1, 1, root)
    couple(2, 2, root)
    anc0[0:units] = root[...]
    anc1[0:units] = root[...]
    solve([1, 2], [3, 4])
    share([1, 2])
    share_end(1)
    couple(3, 5, anc0)
    couple(4, 6, anc0)
    share_end(2)
    couple(5, 7, anc1)
    couple(6, 8, anc1)
    solve([3, 4, 5, 6], [9, 10, 11, 12])

    def exchange(hop):
        return pltpu.make_async_remote_copy(
            src_ref=sums.at[panel],
            dst_ref=sums.at[panel],
            send_sem=sums_send.at[hop],
            recv_sem=sums_recv.at[hop],
            device_id={"panel": lax.rem(panel + hop, panels)},
            device_id_type=MESH,
        )

    for hop in range(1, panels):
        exchange(hop).start()

    @pl.loop(z, depth)
    def _(layer):
        for front in range(7):
            pl.when(has_down)(lambda: transfer(front, layer, y, DOWN).wait_send())
            transfer(front, layer, y, SIDE).wait_send()

    @pl.loop(0, depth)
    def _(layer):
        for gather in range(7, 10):
            pl.when(has_down & (layer >= z))(lambda: transfer(gather, layer, y, DOWN).wait_send())
            pl.when(has_up & (layer <= z))(lambda: transfer(gather, layer, y, UP).wait_send())
            transfer(gather, layer, y, SIDE).wait_send()

    for hop in range(1, panels):
        exchange(hop).wait()
    total = sums[0]
    for i in range(1, panels):
        total = total + sums[i]
    power[...] = total[0:7] / jnp.float32(total_columns)


def local(leaves, panels, right_sides, inverse_diagonal, off_diagonal, structure, pivot_counts):
    fronts, rows, columns = right_sides.shape
    pivots = inverse_diagonal.shape[2]
    coupled = off_diagonal.shape[2]
    unit = math.gcd(rows, coupled // structure.shape[1])
    bf16, f32 = jnp.bfloat16, jnp.float32
    vmem = pl.BlockSpec(memory_space=pltpu.VMEM)
    smem = pl.BlockSpec(memory_space=pltpu.SMEM)
    anywhere = pl.BlockSpec(memory_space=pl.ANY)
    return pl.pallas_call(
        functools.partial(kernel, leaves, panels, columns * panels),
        out_shape=(
            jax.ShapeDtypeStruct((fronts, rows, columns), f32),
            jax.ShapeDtypeStruct((fronts, rows), f32),
        ),
        in_specs=[vmem, anywhere, anywhere, smem, smem],
        out_specs=(vmem, vmem),
        scratch_shapes=[
            pltpu.VMEM((7, pivots, columns), bf16),
            pltpu.VMEM((pivots // unit, unit, columns), bf16),
            pltpu.VMEM((2 * pivots // unit, unit, columns), bf16),
            pltpu.VMEM((2 * pivots // unit, unit, columns), bf16),
            pltpu.VMEM((SLOTS, rows, max(pivots, coupled)), bf16),
            pltpu.VMEM((coupled, columns), bf16),
            pltpu.VMEM((4, rows, columns), f32),
            pltpu.VMEM((panels, 8, rows), f32),
            pltpu.SemaphoreType.DMA((SLOTS,)),
            pltpu.SemaphoreType.DMA((10, 3, leaves // 2)),
            pltpu.SemaphoreType.DMA((10, leaves)),
            pltpu.SemaphoreType.DMA((panels,)),
            pltpu.SemaphoreType.DMA((panels,)),
        ],
        compiler_params=pltpu.CompilerParams(
            collective_id=0, has_side_effects=True, vmem_limit_bytes=58 * 2**20
        ),
        cost_estimate=pl.CostEstimate(
            flops=13 * 2 * rows * pivots * columns,
            bytes_accessed=13 * 2 * rows * pivots,
            transcendentals=0,
        ),
    )(right_sides, inverse_diagonal, off_diagonal, structure, pivot_counts)


def solution(mesh):
    placed = (P(None, "leaf", "panel"), P(None, "leaf", None), P(None, "leaf", None), P(), P())
    return jax.shard_map(
        functools.partial(local, mesh.shape["leaf"], mesh.shape["panel"]),
        mesh=mesh,
        in_specs=placed,
        out_specs=(P(None, "leaf", "panel"), P(None, "leaf")),
        check_vma=False,
    )
```

time: 418 us -> 139 us (0.33)
  waiting for transfers between devices: 252 us -> 0 us
  Pallas kernels: 0 us -> 135 us
  local copies, waits for them, and re-layouts: 91.2 us -> 3.46 us
  matrix products: 41.7 us -> 0 us
  between operations: 14 us -> 0.65 us
  blocking collectives: 10.5 us -> 0 us
  other arithmetic: 7.43 us -> 0 us
    all_gather x5 -> x0, waiting for transfers between devices: 252 us -> none  [the longest x3 167 us: solve_fronts(): lax.all_gather(reduced, 'leaf', axis=1, tiled=True)]
    pallas_call x0 -> x1, Pallas kernels: none -> 135 us  [local(): pl.pallas_call(functools.partial(kernel, leaves, panels, columns * panels...]
    gather x2 -> x0, local copies, waits for them, and re-layouts: 81.4 us -> none  [the longest x1 57.4 us: local(): jnp.take(ancestors, wanted[2:6], axis=0)]
    dot_general x5 -> x0, matrix products: 41.7 us -> none  [the longest x3 23.2 us: solve_fronts(): jnp.einsum('fij,fjr->fir', inverse, lax.all_gather(reduced, 'leaf', axis=...]
    psum x1 -> x0, blocking collectives: 10.5 us -> none  [local(): squares = lax.psum(jnp.sum(results * results, axis=2), 'panel')]
    all_gather x2 -> x0, local copies, waits for them, and re-layouts: 5.7 us -> none  [share_rows(): return lax.all_gather(stored_rows, 'leaf', axis=1, tiled=True)]
  transfers between devices with their start and end apart: 5 -> 0, of which waited for: 5 -> 0; matrix products, arithmetic and copies ran while one was open for 1% -> 0% of each run, Pallas kernels for 0% -> 0%
where the time goes in v1:
time: 139 us
  Pallas kernels  135 us (97%)
  local copies, waits for them, and re-layouts  3.46 us (2%)
    pallas_call x1, Pallas kernels, local(): pl.pallas_call(functools.partial(kernel, leaves, panels, columns * panels...  135 us
    unnamed x4, local copies, waits for them, and re-layouts  3.46 us

profile of v1, /device:TPU:0, one launch (start us, length us, event | category | flops | bytes accessed | tf_op | source)
XLA Modules:
  0.0 139.3 jit_solution(18342268598656130226)
XLA Ops:
  0.6 135.2 %shard_map.68 = (f32[7,512,128]{2,1,0:T(8,128)}, f32[7,512]{1,0:T(8,128)}) custom-call(f32[7,512,128]{2,1,0:T(8,128)} %rhs.1, bf16[7,512,4096]{2,1,0:T(8,128)(2,1)} %inv.1, bf16[6,512,4096]{2,1,0:T(8,128)(2,1)} %off.1, s32[6,32]{1,0:T(8,128)} %structure.1, s32[7]{0:T(128)} %counts.1), custom_call_target="tpu_custom_call" | custom-call | flops 6979321856 | bytes 54525952 | tf_op jit(solution)/shard_map/pallas_call | solution.py:260
  135.8 0.0 copy-start
  135.8 2.9 %copy.9 = f32[7,512,128]{2,1,0:T(8,128)} copy(f32[7,512,128]{2,1,0:T(8,128)} %get-tuple-element.4) | data formatting | bytes 3670016
  138.7 0.0 copy-done
  138.7 0.6 copy.10
Async XLA Ops:
  135.8 2.9 %copy-start = (f32[7,512]{1,0:T(8,128)S(1)}, f32[7,512]{1,0:T(8,128)}, u32[]{:S(2)}) copy-start(f32[7,512]{1,0:T(8,128)} %get-tuple-element.5) | copy-start | bytes 43012

commit v2 on v1

--- a/solution.py
+++ b/solution.py
@@ -9,6 +9,8 @@
 from jax.sharding import PartitionSpec as P
 
 SLOTS = 8
+CHUNKS = 2
+CROSSING = 1
 DOWN, UP, SIDE = 0, 1, 2
 MESH = pl.DeviceIdType.MESH
 
@@ -18,7 +20,7 @@
     rhs, inv, off, structure, counts,
     out, power,
     red, root, anc0, anc1, mats, picked, acc, sums,
-    mat_sem, send_sem, recv_sem, sums_send, sums_recv,
+    mat_sem, send_sem, cross_sem, recv_sem, sums_send, sums_recv,
 ):
     leaf = lax.axis_index("leaf")
     panel = lax.axis_index("panel")
@@ -64,33 +66,60 @@
         greet({"panel": lax.rem(panel + hop, panels)})
     pl.semaphore_wait(barrier, panels + has_down.astype(jnp.int32) + has_up.astype(jnp.int32))
 
-    def rows_of(gather, piece):
+    def rows_of(gather, piece, chunk, chunks=CHUNKS):
+        index = piece * chunks + chunk
         if gather < 7:
-            return red.at[gather, pl.ds(pl.multiple_of(piece * rows, rows), rows)]
+            size = rows // chunks
+            return red.at[gather, pl.ds(pl.multiple_of(index * size, size), size)]
+        size = piece_units // chunks
         if gather == 7:
-            return root.at[pl.ds(piece * piece_units, piece_units)]
-        return (anc0, anc1)[gather - 8].at[pl.ds(units + piece * piece_units, piece_units)]
-
-    def transfer(gather, layer, side, way):
+            return root.at[pl.ds(index * size, size)]
+        return (anc0, anc1)[gather - 8].at[pl.ds(units + index * size, size)]
+
+    def transfer(gather, layer, side, chunk, way, cross=False):
         piece = 2 * layer + side
-        held = rows_of(gather, piece)
+        held = rows_of(gather, piece, chunk)
+        place = layer * CHUNKS + chunk
         return pltpu.make_async_remote_copy(
             src_ref=held,
             dst_ref=held,
-            send_sem=send_sem.at[gather, way, layer],
-            recv_sem=recv_sem.at[gather, piece],
+            send_sem=cross_sem.at[gather, way, chunk] if cross else send_sem.at[gather, way, place],
+            recv_sem=recv_sem.at[gather, piece * CHUNKS + chunk],
             device_id={"leaf": (below, above, beside)[way]},
             device_id_type=MESH,
         )
 
-    def send(gather, layer, way, allowed=None):
-        if allowed is None:
-            transfer(gather, layer, y, way).start()
-        else:
-            pl.when(allowed)(lambda: transfer(gather, layer, y, way).start())
-
-    def arrived(gather, layer, side):
-        transfer(gather, layer, side, SIDE).wait_recv()
+    first_cross = CHUNKS - CROSSING
+
+    def send(gather, layer, chunk, way):
+        transfer(gather, layer, y, chunk, way).start()
+
+    def arrived(gather, layer, side, chunk):
+        transfer(gather, layer, side, chunk, SIDE).wait_recv()
+
+    def relay(gather, layer, way, allowed):
+        for chunk in range(CHUNKS):
+            arrived(gather, layer, y, chunk)
+            pl.when(allowed)(lambda: send(gather, layer, chunk, way))
+            if chunk < first_cross:
+                send(gather, layer, chunk, SIDE)
+            else:
+                near = (layer == z - 1) | (layer == z + 1)
+                pl.when(jnp.logical_not(near))(lambda: send(gather, layer, chunk, SIDE))
+
+    def cross(gather, upward):
+        for chunk in range(first_cross, CHUNKS):
+            arrived(gather, z, 1 - y, chunk)
+            if upward:
+                pl.when(has_up)(lambda: transfer(gather, z, 1 - y, chunk, UP, True).start())
+            pl.when(has_down)(lambda: transfer(gather, z, 1 - y, chunk, DOWN, True).start())
+
+    def publish(gather, upward):
+        for chunk in range(CHUNKS):
+            if upward:
+                pl.when(has_up)(lambda: send(gather, z, chunk, UP))
+            pl.when(has_down)(lambda: send(gather, z, chunk, DOWN))
+            send(gather, z, chunk, SIDE)
 
     position = leaf * rows + lax.broadcasted_iota(jnp.int32, (rows, columns), 0)
 
@@ -99,9 +128,8 @@
 
     def publish_reduced(front, update):
         value = rhs[front] if update is None else rhs[front] - update
-        rows_of(front, leaf)[...] = (live(front) * value).astype(jnp.bfloat16)
-        send(front, z, DOWN, has_down)
-        send(front, z, SIDE)
+        rows_of(front, leaf, 0, 1)[...] = (live(front) * value).astype(jnp.bfloat16)
+        publish(front, False)
 
     def couple(front, order, ancestors):
         parts = block // unit
@@ -132,10 +160,8 @@
         out[front] = solved
         if front < 3:
             gather = 7 + front
-            rows_of(gather, leaf)[...] = solved.astype(jnp.bfloat16).reshape(piece_units, unit, columns)
-            send(gather, z, DOWN, has_down)
-            send(gather, z, UP, has_up)
-            send(gather, z, SIDE)
+            rows_of(gather, leaf, 0, 1)[...] = solved.astype(jnp.bfloat16).reshape(piece_units, unit, columns)
+            publish(gather, True)
         tall = min(rows, 128)
         for i in range(rows // tall):
             part = solved[i * tall:(i + 1) * tall]
@@ -151,17 +177,21 @@
         def _(step):
             layer = z + step
 
-            @pl.when(layer < depth)
-            def _():
-                for front in fronts:
-                    arrived(front, layer, y)
-                    send(front, layer, DOWN, has_down)
-                    send(front, layer, SIDE)
+            for front in fronts:
+                pl.when(layer < depth)(lambda: relay(front, layer, DOWN, has_down))
+                pl.when(step == 1)(lambda: cross(front, False))
 
             done = layer - 1
             start = pl.multiple_of(done * pair, pair)
             for front, order in zip(fronts, orders):
-                arrived(front, done, 1 - y)
+                for chunk in range(first_cross):
+                    arrived(front, done, 1 - y, chunk)
+
+                @pl.when(done > z)
+                def _():
+                    for chunk in range(first_cross, CHUNKS):
+                        arrived(front, done, 1 - y, chunk)
+
                 pl.when(step == 1)(lambda: load(order).wait())
                 acc[front % 4] += jnp.dot(
                     mats[order % SLOTS, :, pl.ds(start, pair)],
@@ -174,27 +204,29 @@
             release(order)
 
     def share(fronts):
-        @pl.loop(1, depth)
+        @pl.loop(z + 1, depth)
+        def _(layer):
+            for front in fronts:
+                relay(7 + front, layer, DOWN, has_down)
+
+        for front in fronts:
+            cross(7 + front, True)
+
+        @pl.loop(1, z + 1)
         def _(step):
             for front in fronts:
-                gather = 7 + front
-
-                @pl.when(z + step < depth)
-                def _():
-                    arrived(gather, z + step, y)
-                    send(gather, z + step, DOWN, has_down)
-                    send(gather, z + step, SIDE)
-
-                @pl.when(z - step >= 0)
-                def _():
-                    arrived(gather, z - step, y)
-                    send(gather, z - step, UP, has_up)
-                    send(gather, z - step, SIDE)
+                relay(7 + front, z - step, UP, has_up)
 
     def share_end(front):
         @pl.loop(0, depth)
         def _(layer):
-            arrived(7 + front, layer, 1 - y)
+            for chunk in range(first_cross):
+                arrived(7 + front, layer, 1 - y, chunk)
+
+            @pl.when(layer != z)
+            def _():
+                for chunk in range(first_cross, CHUNKS):
+                    arrived(7 + front, layer, 1 - y, chunk)
 
     publish_reduced(0, None)
     solve([0], [0])
@@ -227,18 +259,30 @@
     for hop in range(1, panels):
         exchange(hop).start()
 
-    @pl.loop(z, depth)
-    def _(layer):
-        for front in range(7):
-            pl.when(has_down)(lambda: transfer(front, layer, y, DOWN).wait_send())
-            transfer(front, layer, y, SIDE).wait_send()
+    def left(gather, layer, chunk, way, allowed=None):
+        if allowed is None:
+            transfer(gather, layer, y, chunk, way).wait_send()
+        else:
+            pl.when(allowed)(lambda: transfer(gather, layer, y, chunk, way).wait_send())
 
     @pl.loop(0, depth)
     def _(layer):
-        for gather in range(7, 10):
-            pl.when(has_down & (layer >= z))(lambda: transfer(gather, layer, y, DOWN).wait_send())
-            pl.when(has_up & (layer <= z))(lambda: transfer(gather, layer, y, UP).wait_send())
-            transfer(gather, layer, y, SIDE).wait_send()
+        near = (layer == z - 1) | (layer == z + 1)
+        for gather in range(10):
+            for chunk in range(CHUNKS):
+                sideways = layer >= 0 if gather >= 7 else layer >= z
+                if chunk >= first_cross:
+                    sideways = sideways & jnp.logical_not(near)
+                left(gather, layer, chunk, SIDE, sideways)
+                left(gather, layer, chunk, DOWN, has_down & (layer >= z))
+                if gather >= 7:
+                    left(gather, layer, chunk, UP, has_up & (layer <= z))
+
+    for gather in range(10):
+        for chunk in range(first_cross, CHUNKS):
+            pl.when(has_down)(lambda: transfer(gather, z, 1 - y, chunk, DOWN, True).wait_send())
+            if gather >= 7:
+                pl.when(has_up)(lambda: transfer(gather, z, 1 - y, chunk, UP, True).wait_send())
 
     for hop in range(1, panels):
         exchange(hop).wait()
@@ -252,7 +296,7 @@
     fronts, rows, columns = right_sides.shape
     pivots = inverse_diagonal.shape[2]
     coupled = off_diagonal.shape[2]
-    unit = math.gcd(rows, coupled // structure.shape[1])
+    unit = math.gcd(rows // CHUNKS, coupled // structure.shape[1])
     bf16, f32 = jnp.bfloat16, jnp.float32
     vmem = pl.BlockSpec(memory_space=pltpu.VMEM)
     smem = pl.BlockSpec(memory_space=pltpu.SMEM)
@@ -275,8 +319,9 @@
             pltpu.VMEM((4, rows, columns), f32),
             pltpu.VMEM((panels, 8, rows), f32),
             pltpu.SemaphoreType.DMA((SLOTS,)),
-            pltpu.SemaphoreType.DMA((10, 3, leaves // 2)),
-            pltpu.SemaphoreType.DMA((10, leaves)),
+            pltpu.SemaphoreType.DMA((10, 3, CHUNKS * leaves // 2)),
+            pltpu.SemaphoreType.DMA((10, 2, CHUNKS)),
+            pltpu.SemaphoreType.DMA((10, CHUNKS * leaves)),
             pltpu.SemaphoreType.DMA((panels,)),
             pltpu.SemaphoreType.DMA((panels,)),
         ],

time: 139 us -> 128 us (0.921)
  Pallas kernels: 135 us -> 124 us
    pallas_call x1, Pallas kernels: 135 us -> 124 us  [local(): pl.pallas_call(functools.partial(kernel, leaves, panels, columns * panels...]
where the time goes in v2:
time: 128 us
  Pallas kernels  124 us (97%)
  local copies, waits for them, and re-layouts  3.46 us (3%)
    pallas_call x1, Pallas kernels, local(): pl.pallas_call(functools.partial(kernel, leaves, panels, columns * panels...  124 us
    unnamed x4, local copies, waits for them, and re-layouts  3.46 us

profile of v2, /device:TPU:0, one launch (start us, length us, event | category | flops | bytes accessed | tf_op | source)
XLA Modules:
  0.0 128.3 jit_solution(17702450210393762803)
XLA Ops:
  0.6 124.2 %shard_map.68 = (f32[7,512,128]{2,1,0:T(8,128)}, f32[7,512]{1,0:T(8,128)}) custom-call(f32[7,512,128]{2,1,0:T(8,128)} %rhs.1, bf16[7,512,4096]{2,1,0:T(8,128)(2,1)} %inv.1, bf16[6,512,4096]{2,1,0:T(8,128)(2,1)} %off.1, s32[6,32]{1,0:T(8,128)} %structure.1, s32[7]{0:T(128)} %counts.1), custom_call_target="tpu_custom_call" | custom-call | flops 6979321856 | bytes 54525952 | tf_op jit(solution)/shard_map/pallas_call | solution.py:304
  124.8 0.0 copy-start
  124.8 2.9 %copy.9 = f32[7,512,128]{2,1,0:T(8,128)} copy(f32[7,512,128]{2,1,0:T(8,128)} %get-tuple-element.4) | data formatting | bytes 3670016
  127.7 0.0 copy-done
  127.7 0.6 copy.10
Async XLA Ops:
  124.8 2.9 %copy-start = (f32[7,512]{1,0:T(8,128)S(1)}, f32[7,512]{1,0:T(8,128)}, u32[]{:S(2)}) copy-start(f32[7,512]{1,0:T(8,128)} %get-tuple-element.5) | copy-start | bytes 43012

commit v3 on v2

--- a/solution.py
+++ b/solution.py
@@ -8,19 +8,23 @@
 from jax.experimental.pallas import tpu as pltpu
 from jax.sharding import PartitionSpec as P
 
-SLOTS = 8
-CHUNKS = 2
-CROSSING = 1
+SLOTS = 7
+HELPED = (3, 4)
 DOWN, UP, SIDE = 0, 1, 2
 MESH = pl.DeviceIdType.MESH
+
+
+def share_chunks(rows):
+    return max(2, min(4, rows // 32))
 
 
 def kernel(
     leaves, panels, total_columns,
     rhs, inv, off, structure, counts,
     out, power,
-    red, root, anc0, anc1, mats, picked, acc, sums,
+    red, root, anc0, anc1, mats, picked, acc, sums, lent, helping, part,
     mat_sem, send_sem, cross_sem, recv_sem, sums_send, sums_recv,
+    lend_send, lend_recv, share_send, part_send, part_recv,
 ):
     leaf = lax.axis_index("leaf")
     panel = lax.axis_index("panel")
@@ -34,6 +38,10 @@
     pair = 2 * rows
     wide = min(coupled, 1024)
     unit = root.shape[1]
+
+    def chunks_of(gather):
+        return 2 if gather < 7 else share_chunks(rows)
+
     units, piece_units = pivots // unit, rows // unit
 
     sequence = [(inv, 0), (off, 0), (off, 1), (inv, 1), (inv, 2)]
@@ -66,7 +74,7 @@
         greet({"panel": lax.rem(panel + hop, panels)})
     pl.semaphore_wait(barrier, panels + has_down.astype(jnp.int32) + has_up.astype(jnp.int32))
 
-    def rows_of(gather, piece, chunk, chunks=CHUNKS):
+    def rows_of(gather, piece, chunk, chunks):
         index = piece * chunks + chunk
         if gather < 7:
             size = rows // chunks
@@ -78,47 +86,49 @@
 
     def transfer(gather, layer, side, chunk, way, cross=False):
         piece = 2 * layer + side
-        held = rows_of(gather, piece, chunk)
-        place = layer * CHUNKS + chunk
+        chunks = chunks_of(gather)
+        held = rows_of(gather, piece, chunk, chunks)
+        place = layer * chunks + chunk
         return pltpu.make_async_remote_copy(
             src_ref=held,
             dst_ref=held,
             send_sem=cross_sem.at[gather, way, chunk] if cross else send_sem.at[gather, way, place],
-            recv_sem=recv_sem.at[gather, piece * CHUNKS + chunk],
+            recv_sem=recv_sem.at[gather, piece * chunks + chunk],
             device_id={"leaf": (below, above, beside)[way]},
             device_id_type=MESH,
         )
 
-    first_cross = CHUNKS - CROSSING
-
     def send(gather, layer, chunk, way):
         transfer(gather, layer, y, chunk, way).start()
 
     def arrived(gather, layer, side, chunk):
         transfer(gather, layer, side, chunk, SIDE).wait_recv()
 
-    def relay(gather, layer, way, allowed):
-        for chunk in range(CHUNKS):
+    def sinks(gather):
+        return z > 1 if gather in HELPED else has_down
+
+    def relay(gather, layer, way):
+        for chunk in range(chunks_of(gather)):
             arrived(gather, layer, y, chunk)
-            pl.when(allowed)(lambda: send(gather, layer, chunk, way))
-            if chunk < first_cross:
+            pl.when(has_up if way == UP else sinks(gather))(lambda: send(gather, layer, chunk, way))
+            if chunk < chunks_of(gather) // 2:
                 send(gather, layer, chunk, SIDE)
             else:
                 near = (layer == z - 1) | (layer == z + 1)
                 pl.when(jnp.logical_not(near))(lambda: send(gather, layer, chunk, SIDE))
 
     def cross(gather, upward):
-        for chunk in range(first_cross, CHUNKS):
+        for chunk in range(chunks_of(gather) // 2, chunks_of(gather)):
             arrived(gather, z, 1 - y, chunk)
             if upward:
                 pl.when(has_up)(lambda: transfer(gather, z, 1 - y, chunk, UP, True).start())
-            pl.when(has_down)(lambda: transfer(gather, z, 1 - y, chunk, DOWN, True).start())
+            pl.when(sinks(gather))(lambda: transfer(gather, z, 1 - y, chunk, DOWN, True).start())
 
     def publish(gather, upward):
-        for chunk in range(CHUNKS):
+        for chunk in range(chunks_of(gather)):
             if upward:
                 pl.when(has_up)(lambda: send(gather, z, chunk, UP))
-            pl.when(has_down)(lambda: send(gather, z, chunk, DOWN))
+            pl.when(sinks(gather))(lambda: send(gather, z, chunk, DOWN))
             send(gather, z, chunk, SIDE)
 
     position = leaf * rows + lax.broadcasted_iota(jnp.int32, (rows, columns), 0)
@@ -155,7 +165,70 @@
         release(order)
         publish_reduced(front, acc[0])
 
+    share_rows = rows // panels
+
+    def lent_rows(i, quarter):
+        return lent.at[i, pl.ds(pl.multiple_of(quarter * share_rows, share_rows), share_rows)]
+
+    def lend(i):
+        taken = pl.ds(pl.multiple_of(panel * share_rows, share_rows), share_rows)
+        return pltpu.make_async_remote_copy(
+            src_ref=inv.at[HELPED[i], taken, pl.ds(pair, pivots - pair)],
+            dst_ref=lent_rows(i, panel),
+            send_sem=lend_send.at[i],
+            recv_sem=lend_recv.at[i, 0],
+            device_id={"leaf": above},
+            device_id_type=MESH,
+        )
+
+    def pass_on(i, hop):
+        return pltpu.make_async_remote_copy(
+            src_ref=lent_rows(i, panel),
+            dst_ref=lent_rows(i, panel),
+            send_sem=share_send.at[i, hop],
+            recv_sem=lend_recv.at[i, hop],
+            device_id={"panel": lax.rem(panel + hop, panels)},
+            device_id_type=MESH,
+        )
+
+    def lend_out(i):
+        pl.when(z == 0)(lambda: lend(i).start())
+
+    def pass_around(i):
+        @pl.when(z == 1)
+        def _():
+            lend(i).wait_recv()
+            for hop in range(1, panels):
+                pass_on(i, hop).start()
+
+    def lent_here(i):
+        @pl.when(z == 1)
+        def _():
+            for hop in range(1, panels):
+                pass_on(i, hop).wait()
+            helping[i] = jnp.zeros((rows, columns), jnp.float32)
+
+        pl.when(z == 0)(lambda: lend(i).wait_send())
+
+    def hand(i):
+        return pltpu.make_async_remote_copy(
+            src_ref=part.at[i],
+            dst_ref=part.at[i],
+            send_sem=part_send.at[i],
+            recv_sem=part_recv.at[i],
+            device_id={"leaf": below},
+            device_id_type=MESH,
+        )
+
     def finish(front):
+        if front in HELPED:
+            i = HELPED.index(front)
+
+            @pl.when(z == 0)
+            def _():
+                hand(i).wait_recv()
+                acc[front % 4] += part[i].astype(jnp.float32)
+
         solved = live(front) * acc[front % 4]
         out[front] = solved
         if front < 3:
@@ -164,9 +237,9 @@
             publish(gather, True)
         tall = min(rows, 128)
         for i in range(rows // tall):
-            part = solved[i * tall:(i + 1) * tall]
+            strip = solved[i * tall:(i + 1) * tall]
             sums[panel, pl.ds(front, 1), i * tall:(i + 1) * tall] = jnp.sum(
-                (part * part).T, axis=0, keepdims=True
+                (strip * strip).T, axis=0, keepdims=True
             )
 
     def solve(fronts, orders):
@@ -178,18 +251,21 @@
             layer = z + step
 
             for front in fronts:
-                pl.when(layer < depth)(lambda: relay(front, layer, DOWN, has_down))
+                more = layer < depth
+                if front in HELPED:
+                    more = more & (z > 0)
+                pl.when(more)(lambda: relay(front, layer, DOWN))
                 pl.when(step == 1)(lambda: cross(front, False))
 
             done = layer - 1
             start = pl.multiple_of(done * pair, pair)
-            for front, order in zip(fronts, orders):
-                for chunk in range(first_cross):
+            def gain(front, order):
+                for chunk in range(chunks_of(front) // 2):
                     arrived(front, done, 1 - y, chunk)
 
                 @pl.when(done > z)
                 def _():
-                    for chunk in range(first_cross, CHUNKS):
+                    for chunk in range(chunks_of(front) // 2, chunks_of(front)):
                         arrived(front, done, 1 - y, chunk)
 
                 pl.when(step == 1)(lambda: load(order).wait())
@@ -198,6 +274,26 @@
                     red[front, pl.ds(start, pair), :],
                     preferred_element_type=jnp.float32,
                 )
+
+            def help_below(front):
+                i = HELPED.index(front)
+                helping[i] += jnp.dot(
+                    lent[i, :, pl.ds(pl.multiple_of(start - pair, pair), pair)],
+                    red[front, pl.ds(start, pair), :],
+                    preferred_element_type=jnp.float32,
+                )
+
+                @pl.when(layer == depth)
+                def _():
+                    part[i] = helping[i].astype(jnp.bfloat16)
+                    hand(i).start()
+
+            for front, order in zip(fronts, orders):
+                if front in HELPED:
+                    pl.when((z > 0) | (done == 0))(lambda: gain(front, order))
+                    pl.when(z == 1)(lambda: help_below(front))
+                else:
+                    gain(front, order)
                 pl.when(layer == depth)(lambda: finish(front))
 
         for order in orders:
@@ -207,7 +303,7 @@
         @pl.loop(z + 1, depth)
         def _(layer):
             for front in fronts:
-                relay(7 + front, layer, DOWN, has_down)
+                relay(7 + front, layer, DOWN)
 
         for front in fronts:
             cross(7 + front, True)
@@ -215,28 +311,32 @@
         @pl.loop(1, z + 1)
         def _(step):
             for front in fronts:
-                relay(7 + front, z - step, UP, has_up)
+                relay(7 + front, z - step, UP)
 
     def share_end(front):
         @pl.loop(0, depth)
         def _(layer):
-            for chunk in range(first_cross):
+            for chunk in range(chunks_of(7 + front) // 2):
                 arrived(7 + front, layer, 1 - y, chunk)
 
             @pl.when(layer != z)
             def _():
-                for chunk in range(first_cross, CHUNKS):
+                for chunk in range(chunks_of(7 + front) // 2, chunks_of(7 + front)):
                     arrived(7 + front, layer, 1 - y, chunk)
 
+    lend_out(0)
     publish_reduced(0, None)
     solve([0], [0])
     share([0])
     share_end(0)
+    lend_out(1)
+    pass_around(0)
     couple(1, 1, root)
     couple(2, 2, root)
     anc0[0:units] = root[...]
     anc1[0:units] = root[...]
     solve([1, 2], [3, 4])
+    pass_around(1)
     share([1, 2])
     share_end(1)
     couple(3, 5, anc0)
@@ -244,6 +344,8 @@
     share_end(2)
     couple(5, 7, anc1)
     couple(6, 8, anc1)
+    lent_here(0)
+    lent_here(1)
     solve([3, 4, 5, 6], [9, 10, 11, 12])
 
     def exchange(hop):
@@ -269,20 +371,25 @@
     def _(layer):
         near = (layer == z - 1) | (layer == z + 1)
         for gather in range(10):
-            for chunk in range(CHUNKS):
+            for chunk in range(chunks_of(gather)):
                 sideways = layer >= 0 if gather >= 7 else layer >= z
-                if chunk >= first_cross:
+                if gather in HELPED:
+                    sideways = sideways & ((z > 0) | (layer == 0))
+                if chunk >= chunks_of(gather) // 2:
                     sideways = sideways & jnp.logical_not(near)
                 left(gather, layer, chunk, SIDE, sideways)
-                left(gather, layer, chunk, DOWN, has_down & (layer >= z))
+                left(gather, layer, chunk, DOWN, sinks(gather) & (layer >= z))
                 if gather >= 7:
                     left(gather, layer, chunk, UP, has_up & (layer <= z))
 
     for gather in range(10):
-        for chunk in range(first_cross, CHUNKS):
-            pl.when(has_down)(lambda: transfer(gather, z, 1 - y, chunk, DOWN, True).wait_send())
+        for chunk in range(chunks_of(gather) // 2, chunks_of(gather)):
+            pl.when(sinks(gather))(lambda: transfer(gather, z, 1 - y, chunk, DOWN, True).wait_send())
             if gather >= 7:
                 pl.when(has_up)(lambda: transfer(gather, z, 1 - y, chunk, UP, True).wait_send())
+
+    for i in range(len(HELPED)):
+        pl.when(z == 1)(lambda: hand(i).wait_send())
 
     for hop in range(1, panels):
         exchange(hop).wait()
@@ -296,7 +403,7 @@
     fronts, rows, columns = right_sides.shape
     pivots = inverse_diagonal.shape[2]
     coupled = off_diagonal.shape[2]
-    unit = math.gcd(rows // CHUNKS, coupled // structure.shape[1])
+    unit = math.gcd(rows // share_chunks(rows), coupled // structure.shape[1])
     bf16, f32 = jnp.bfloat16, jnp.float32
     vmem = pl.BlockSpec(memory_space=pltpu.VMEM)
     smem = pl.BlockSpec(memory_space=pltpu.SMEM)
@@ -318,15 +425,23 @@
             pltpu.VMEM((coupled, columns), bf16),
             pltpu.VMEM((4, rows, columns), f32),
             pltpu.VMEM((panels, 8, rows), f32),
+            pltpu.VMEM((len(HELPED), rows, pivots - 2 * rows), bf16),
+            pltpu.VMEM((len(HELPED), rows, columns), f32),
+            pltpu.VMEM((len(HELPED), rows, columns), bf16),
             pltpu.SemaphoreType.DMA((SLOTS,)),
-            pltpu.SemaphoreType.DMA((10, 3, CHUNKS * leaves // 2)),
-            pltpu.SemaphoreType.DMA((10, 2, CHUNKS)),
-            pltpu.SemaphoreType.DMA((10, CHUNKS * leaves)),
+            pltpu.SemaphoreType.DMA((10, 3, share_chunks(rows) * leaves // 2)),
+            pltpu.SemaphoreType.DMA((10, 2, share_chunks(rows))),
+            pltpu.SemaphoreType.DMA((10, share_chunks(rows) * leaves)),
             pltpu.SemaphoreType.DMA((panels,)),
             pltpu.SemaphoreType.DMA((panels,)),
+            pltpu.SemaphoreType.DMA((len(HELPED),)),
+            pltpu.SemaphoreType.DMA((len(HELPED), panels)),
+            pltpu.SemaphoreType.DMA((len(HELPED), panels)),
+            pltpu.SemaphoreType.DMA((len(HELPED),)),
+            pltpu.SemaphoreType.DMA((len(HELPED),)),
         ],
         compiler_params=pltpu.CompilerParams(
-            collective_id=0, has_side_effects=True, vmem_limit_bytes=58 * 2**20
+            collective_id=0, has_side_effects=True, vmem_limit_bytes=60 * 2**20
         ),
         cost_estimate=pl.CostEstimate(
             flops=13 * 2 * rows * pivots * columns,

time: 128 us -> 135 us (1.055)
  Pallas kernels: 124 us -> 131 us
    pallas_call x1, Pallas kernels: 124 us -> 131 us  [local(): pl.pallas_call(functools.partial(kernel, leaves, panels, columns * panels...]
where the time goes in v3:
time: 135 us
  Pallas kernels  131 us (97%)
  local copies, waits for them, and re-layouts  3.46 us (3%)
    pallas_call x1, Pallas kernels, local(): pl.pallas_call(functools.partial(kernel, leaves, panels, columns * panels...  131 us
    unnamed x4, local copies, waits for them, and re-layouts  3.46 us

profile of v3, /device:TPU:0, one launch (start us, length us, event | category | flops | bytes accessed | tf_op | source)
XLA Modules:
  0.0 134.9 jit_solution(4659405211251279923)
XLA Ops:
  0.6 130.8 %shard_map.68 = (f32[7,512,128]{2,1,0:T(8,128)}, f32[7,512]{1,0:T(8,128)}) custom-call(f32[7,512,128]{2,1,0:T(8,128)} %rhs.1, bf16[7,512,4096]{2,1,0:T(8,128)(2,1)} %inv.1, bf16[6,512,4096]{2,1,0:T(8,128)(2,1)} %off.1, s32[6,32]{1,0:T(8,128)} %structure.1, s32[7]{0:T(128)} %counts.1), custom_call_target="tpu_custom_call" | custom-call | flops 6979321856 | bytes 54525952 | tf_op jit(solution)/shard_map/pallas_call | solution.py:411
  131.4 0.0 copy-start
  131.4 2.9 %copy.9 = f32[7,512,128]{2,1,0:T(8,128)} copy(f32[7,512,128]{2,1,0:T(8,128)} %get-tuple-element.4) | data formatting | bytes 3670016
  134.3 0.0 copy-done
  134.3 0.6 copy.10
Async XLA Ops:
  131.4 2.9 %copy-start = (f32[7,512]{1,0:T(8,128)S(1)}, f32[7,512]{1,0:T(8,128)}, u32[]{:S(2)}) copy-start(f32[7,512]{1,0:T(8,128)} %get-tuple-element.5) | copy-start | bytes 43012

commit v4 on v3

--- a/solution.py
+++ b/solution.py
@@ -15,7 +15,7 @@
 
 
 def share_chunks(rows):
-    return max(2, min(4, rows // 32))
+    return max(2, min(2, rows // 32))
 
 
 def kernel(
@@ -181,32 +181,55 @@
             device_id_type=MESH,
         )
 
-    def pass_on(i, hop):
+    def flip(at, distance):
+        return at + distance - 2 * distance * ((at // distance) % 2)
+
+    distances = []
+    while 2 ** len(distances) < panels:
+        distances.append(panels // 2 ** (len(distances) + 1))
+
+    def pass_on(i, stage, held):
+        distance = distances[stage]
+        quarter = panel
+        for k, other in enumerate(distances[:stage]):
+            if held >> k & 1:
+                quarter = flip(quarter, other)
+        slot = held + 2 ** stage
         return pltpu.make_async_remote_copy(
-            src_ref=lent_rows(i, panel),
-            dst_ref=lent_rows(i, panel),
-            send_sem=share_send.at[i, hop],
-            recv_sem=lend_recv.at[i, hop],
-            device_id={"panel": lax.rem(panel + hop, panels)},
+            src_ref=lent_rows(i, quarter),
+            dst_ref=lent_rows(i, quarter),
+            send_sem=share_send.at[i, slot],
+            recv_sem=lend_recv.at[i, slot],
+            device_id={"panel": flip(panel, distance)},
             device_id_type=MESH,
         )
 
     def lend_out(i):
         pl.when(z == 0)(lambda: lend(i).start())
 
-    def pass_around(i):
+    def pass_around(i, stage):
         @pl.when(z == 1)
         def _():
-            lend(i).wait_recv()
-            for hop in range(1, panels):
-                pass_on(i, hop).start()
+            if stage == 0:
+                lend(i).wait_recv()
+            else:
+                for held in range(2 ** (stage - 1)):
+                    pass_on(i, stage - 1, held).wait_recv()
+            for held in range(2 ** stage):
+                pass_on(i, stage, held).start()
 
     def lent_here(i):
+        for held in range(2 ** (len(distances) - 1)):
+            pass_on(i, len(distances) - 1, held).wait_recv()
+        helping[i] = jnp.zeros((rows, columns), jnp.float32)
+
+    def lent_left(i):
         @pl.when(z == 1)
         def _():
-            for hop in range(1, panels):
-                pass_on(i, hop).wait()
-            helping[i] = jnp.zeros((rows, columns), jnp.float32)
+            for stage in range(len(distances)):
+                for held in range(2 ** stage):
+                    pass_on(i, stage, held).wait_send()
+            hand(i).wait_send()
 
         pl.when(z == 0)(lambda: lend(i).wait_send())
 
@@ -277,6 +300,7 @@
 
             def help_below(front):
                 i = HELPED.index(front)
+                pl.when(step == 1)(lambda: lent_here(i))
                 helping[i] += jnp.dot(
                     lent[i, :, pl.ds(pl.multiple_of(start - pair, pair), pair)],
                     red[front, pl.ds(start, pair), :],
@@ -324,28 +348,31 @@
                 for chunk in range(chunks_of(7 + front) // 2, chunks_of(7 + front)):
                     arrived(7 + front, layer, 1 - y, chunk)
 
+    stages = len(distances)
     lend_out(0)
     publish_reduced(0, None)
     solve([0], [0])
     share([0])
     share_end(0)
     lend_out(1)
-    pass_around(0)
+    pass_around(0, 0)
     couple(1, 1, root)
     couple(2, 2, root)
     anc0[0:units] = root[...]
     anc1[0:units] = root[...]
     solve([1, 2], [3, 4])
-    pass_around(1)
+    for stage in range(1, stages):
+        pass_around(0, stage)
+    pass_around(1, 0)
     share([1, 2])
     share_end(1)
     couple(3, 5, anc0)
     couple(4, 6, anc0)
     share_end(2)
+    for stage in range(1, stages):
+        pass_around(1, stage)
     couple(5, 7, anc1)
     couple(6, 8, anc1)
-    lent_here(0)
-    lent_here(1)
     solve([3, 4, 5, 6], [9, 10, 11, 12])
 
     def exchange(hop):
@@ -389,7 +416,7 @@
                 pl.when(has_up)(lambda: transfer(gather, z, 1 - y, chunk, UP, True).wait_send())
 
     for i in range(len(HELPED)):
-        pl.when(z == 1)(lambda: hand(i).wait_send())
+        lent_left(i)
 
     for hop in range(1, panels):
         exchange(hop).wait()

time: 135 us -> 121 us (0.90)
  Pallas kernels: 131 us -> 117 us
    pallas_call x1, Pallas kernels: 131 us -> 117 us  [local(): pl.pallas_call(functools.partial(kernel, leaves, panels, columns * panels...]
where the time goes in v4:
time: 121 us
  Pallas kernels  117 us (97%)
  local copies, waits for them, and re-layouts  3.46 us (3%)
    pallas_call x1, Pallas kernels, local(): pl.pallas_call(functools.partial(kernel, leaves, panels, columns * panels...  117 us
    unnamed x4, local copies, waits for them, and re-layouts  3.46 us

profile of v4, /device:TPU:0, one launch (start us, length us, event | category | flops | bytes accessed | tf_op | source)
XLA Modules:
  0.0 121.2 jit_solution(13611250745414456515)
XLA Ops:
  0.6 117.1 %shard_map.68 = (f32[7,512,128]{2,1,0:T(8,128)}, f32[7,512]{1,0:T(8,128)}) custom-call(f32[7,512,128]{2,1,0:T(8,128)} %rhs.1, bf16[7,512,4096]{2,1,0:T(8,128)(2,1)} %inv.1, bf16[6,512,4096]{2,1,0:T(8,128)(2,1)} %off.1, s32[6,32]{1,0:T(8,128)} %structure.1, s32[7]{0:T(128)} %counts.1), custom_call_target="tpu_custom_call" | custom-call | flops 6979321856 | bytes 54525952 | tf_op jit(solution)/shard_map/pallas_call | solution.py:438
  117.8 0.0 copy-start
  117.8 2.9 %copy.9 = f32[7,512,128]{2,1,0:T(8,128)} copy(f32[7,512,128]{2,1,0:T(8,128)} %get-tuple-element.4) | data formatting | bytes 3670016
  120.6 0.0 copy-done
  120.6 0.6 copy.10
Async XLA Ops:
  117.8 2.9 %copy-start = (f32[7,512]{1,0:T(8,128)S(1)}, f32[7,512]{1,0:T(8,128)}, u32[]{:S(2)}) copy-start(f32[7,512]{1,0:T(8,128)} %get-tuple-element.5) | copy-start | bytes 43012

commit v5 on v4

--- a/solution.py
+++ b/solution.py
@@ -15,15 +15,15 @@
 
 
 def share_chunks(rows):
-    return max(2, min(2, rows // 32))
+    return min(2, rows // 16)
 
 
 def kernel(
     leaves, panels, total_columns,
-    rhs, inv, off, structure, counts,
-    out, power,
-    red, root, anc0, anc1, mats, picked, acc, sums, lent, helping, part,
-    mat_sem, send_sem, cross_sem, recv_sem, sums_send, sums_recv,
+    given, inv, off, structure, counts,
+    samples, power,
+    rhs, out, red, root, anc0, anc1, mats, picked, acc, sums, lent, helping, part,
+    given_sem, out_sem, mat_sem, send_sem, cross_sem, recv_sem, sums_send, sums_recv,
     lend_send, lend_recv, share_send, part_send, part_recv,
 ):
     leaf = lax.axis_index("leaf")
@@ -56,8 +56,17 @@
         if i + SLOTS < len(sequence):
             load(i + SLOTS).start()
 
+    def take_in(front):
+        return pltpu.make_async_copy(given.at[front], rhs.at[front], given_sem.at[front])
+
+    def put_out(front):
+        return pltpu.make_async_copy(out.at[front], samples.at[front], out_sem.at[front])
+
+    take_in(0).start()
     for i in range(min(SLOTS, len(sequence))):
         load(i).start()
+    for front in range(1, 7):
+        take_in(front).start()
 
     has_down, has_up = z > 0, z < depth - 1
 
@@ -137,6 +146,7 @@
         return jnp.clip(counts[front] - position, 0, 1).astype(jnp.float32)
 
     def publish_reduced(front, update):
+        take_in(front).wait()
         value = rhs[front] if update is None else rhs[front] - update
         rows_of(front, leaf, 0, 1)[...] = (live(front) * value).astype(jnp.bfloat16)
         publish(front, False)
@@ -253,11 +263,12 @@
                 acc[front % 4] += part[i].astype(jnp.float32)
 
         solved = live(front) * acc[front % 4]
-        out[front] = solved
         if front < 3:
             gather = 7 + front
             rows_of(gather, leaf, 0, 1)[...] = solved.astype(jnp.bfloat16).reshape(piece_units, unit, columns)
             publish(gather, True)
+        out[front] = solved
+        put_out(front).start()
         tall = min(rows, 128)
         for i in range(rows // tall):
             strip = solved[i * tall:(i + 1) * tall]
@@ -420,6 +431,8 @@
 
     for hop in range(1, panels):
         exchange(hop).wait()
+    for front in range(7):
+        put_out(front).wait()
     total = sums[0]
     for i in range(1, panels):
         total = total + sums[i]
@@ -441,9 +454,11 @@
             jax.ShapeDtypeStruct((fronts, rows, columns), f32),
             jax.ShapeDtypeStruct((fronts, rows), f32),
         ),
-        in_specs=[vmem, anywhere, anywhere, smem, smem],
-        out_specs=(vmem, vmem),
+        in_specs=[anywhere, anywhere, anywhere, smem, smem],
+        out_specs=(anywhere, vmem),
         scratch_shapes=[
+            pltpu.VMEM((fronts, rows, columns), f32),
+            pltpu.VMEM((fronts, rows, columns), f32),
             pltpu.VMEM((7, pivots, columns), bf16),
             pltpu.VMEM((pivots // unit, unit, columns), bf16),
             pltpu.VMEM((2 * pivots // unit, unit, columns), bf16),
@@ -455,6 +470,8 @@
             pltpu.VMEM((len(HELPED), rows, pivots - 2 * rows), bf16),
             pltpu.VMEM((len(HELPED), rows, columns), f32),
             pltpu.VMEM((len(HELPED), rows, columns), bf16),
+            pltpu.SemaphoreType.DMA((fronts,)),
+            pltpu.SemaphoreType.DMA((fronts,)),
             pltpu.SemaphoreType.DMA((SLOTS,)),
             pltpu.SemaphoreType.DMA((10, 3, share_chunks(rows) * leaves // 2)),
             pltpu.SemaphoreType.DMA((10, 2, share_chunks(rows))),

time: 121 us -> 121 us (level)
  no operation moved by 1% of the time
where the time goes in v5:
time: 121 us
  Pallas kernels  117 us (97%)
  local copies, waits for them, and re-layouts  3.46 us (3%)
    pallas_call x1, Pallas kernels, local(): pl.pallas_call(functools.partial(kernel, leaves, panels, columns * panels...  117 us
    unnamed x4, local copies, waits for them, and re-layouts  3.46 us

profile of v5, /device:TPU:0, one launch (start us, length us, event | category | flops | bytes accessed | tf_op | source)
XLA Modules:
  0.0 120.8 jit_solution(14199874817340558071)
XLA Ops:
  0.6 116.7 %shard_map.68 = (f32[7,512,128]{2,1,0:T(8,128)}, f32[7,512]{1,0:T(8,128)}) custom-call(f32[7,512,128]{2,1,0:T(8,128)} %given.1, bf16[7,512,4096]{2,1,0:T(8,128)(2,1)} %inv.1, bf16[6,512,4096]{2,1,0:T(8,128)(2,1)} %off.1, s32[6,32]{1,0:T(8,128)} %structure.1, s32[7]{0:T(128)} %counts.1), custom_call_target="tpu_custom_call" | custom-call | flops 6979321856 | bytes 54525952 | tf_op jit(solution)/shard_map/pallas_call | solution.py:451
  117.3 0.0 copy-start
  117.3 2.9 %copy.9 = f32[7,512,128]{2,1,0:T(8,128)} copy(f32[7,512,128]{2,1,0:T(8,128)} %get-tuple-element.4) | data formatting | bytes 3670016
  120.2 0.0 copy-done
  120.2 0.6 copy.10
Async XLA Ops:
  117.3 2.9 %copy-start = (f32[7,512]{1,0:T(8,128)S(1)}, f32[7,512]{1,0:T(8,128)}, u32[]{:S(2)}) copy-start(f32[7,512]{1,0:T(8,128)} %get-tuple-element.5) | copy-start | bytes 43012
